TPU v7x, 32 devices: a whole 2x2x4 slice. The times are simulated.
32 devices in a mesh: row: 2 (over x), col: 4 (over y, core), layer: 4 (over z).
Axes of the slice: x: 2, y: 2, z: 4, core: 2. Of those that a mesh axis runs over, the one named last changes fastest.
Arguments:
- front: float32 [8192, 8192], P('row', ('col', 'layer')), may hold values from -8 to 256, as said below
Outputs:
- eliminated: float32 [8192, 8192], P('row', ('col', 'layer'))
Inputs may be any that keep to these rules, and one draw needn't show every extreme that they name: `front`: every pivot block met during the elimination has a nonzero diagonal, and the Newton-Schulz iteration started from the inverse of its diagonal converges.
All inputs are finite; a program needn't handle non-finite values.
Results may differ from a plain program's by a relative error of at most 0.0001.
Values sent between devices are 32-bit elements; how exact they have to be, the bound alone decides.
A program may use at most 128 MiB of HBM per device.

v0:
```python
import jax
import jax.numpy as jnp
from jax import lax
from jax.sharding import PartitionSpec as P

B = 64
ITERS = 2
P_SIZE = 256


def spread(x, axis, root):
    mine = lax.axis_index(axis) == root
    return lax.psum(jnp.where(mine, x, jnp.zeros_like(x)), axis)


def exact_dot(left, right):
    return jnp.dot(left, right, precision=lax.Precision.HIGHEST, preferred_element_type=jnp.float32)


def newton_inverse(pivot):
    inverse = jnp.diag(1.0 / jnp.diagonal(pivot))
    for sweep in range(ITERS):
        inverse = 2.0 * inverse - exact_dot(inverse, exact_dot(pivot, inverse))
    return inverse


def lower_rows(inverse, column_slab):
    return lax.dot_general(
        inverse,
        column_slab,
        (((0,), (1,)), ((), ())),
        precision=lax.Precision.HIGHEST,
        preferred_element_type=jnp.float32,
    )


def trailing_drop(lower_used, upper_used):
    return lax.dot_general(
        lower_used,
        upper_used,
        (((0,), (0,)), ((), ())),
        precision=lax.Precision.HIGHEST,
        preferred_element_type=jnp.float32,
    )


def per_device(front):
    row_count, width = front.shape
    row_index = lax.axis_index("row") * row_count + jnp.arange(row_count, dtype=jnp.int32)
    flat_pos = lax.axis_index("col") * lax.axis_size("layer") + lax.axis_index("layer")
    col_index = flat_pos * width + jnp.arange(width, dtype=jnp.int32)
    share = front
    carried = None
    block_total = P_SIZE // B
    for block in range(block_total):
        block_begin = block * B
        block_end = block_begin + B
        root = block_begin // width
        offset = block_begin % width
        owner = flat_pos == root
        column_slab = share[:, offset : offset + B]
        row_slab = share[block_begin:block_end, :]
        upper = spread(row_slab, "row", 0)
        pivot = jnp.where(owner, upper[:, offset : offset + B], jnp.eye(B, dtype=jnp.float32))
        inverse = newton_inverse(pivot)
        lower_t = spread(lower_rows(inverse, column_slab), ("col", "layer"), root)
        below = row_index >= block_end
        after = col_index >= block_end
        lower_used = jnp.where(below[None, :], lower_t, 0.0)
        upper_used = jnp.where(after[None, :], upper, 0.0)
        share = share - trailing_drop(lower_used, upper_used)
        carried = None
        new_column = jnp.where(below[:, None], lower_t.T, column_slab)
        new_column = jnp.where(owner, new_column, share[:, offset : offset + B])
        share = share.at[:, offset : offset + B].set(new_column)
    return share


def solution(mesh):
    placed = (P("row", ("col", "layer")),)
    return jax.shard_map(
        per_device,
        mesh=mesh,
        in_specs=placed,
        out_specs=P("row", ("col", "layer")),
        check_vma=False,
    )
```

profile of v0, /device:TPU:27, one launch (start us, length us, event | category | flops | bytes accessed | tf_op | source)
XLA Modules:
  0.0 638.6 jit_solution(11131925160351621203)
XLA Ops:
  8.2 22.5 %all-reduce.9.cloned.1.call-done = f32[64,512]{1,0:T(8,128)} async-done(((f32[64,512]{1,0:T(8,128)}), f32[64,512]{1,0:T(8,128)}) %all-reduce.9.cloned.1.call-update) | async-done | bytes 131088 | tf_op jit(solution)/shard_map/psum | solution.py:13
  33.1 4.7 convolution_select_fusion.3
  38.6 96.3 %all-reduce.11.cloned.1.call-done = f32[64,4096]{0,1:T(8,128)} async-done(((f32[64,4096]{0,1:T(8,128)}), f32[64,4096]{0,1:T(8,128)}) %all-reduce.11.cloned.1.call-update) | async-done | bytes 1048592 | tf_op jit(solution)/shard_map/psum | solution.py:13
  134.8 9.6 %convolution_subtract_fusion.3 = f32[4096,512]{1,0:T(8,128)S(1)} fusion(f32[4096,512]{1,0:T(8,128)} %param.9, f32[64,4096]{0,1:T(8,128)} %all-reduce.11.cloned.1.call-done, pred[4096]{0:T(1024)(128)(4,1)S(1)} %fusion.59, f32[64,512]{1,0:T(8,128)S(1)} %copy-done.8, pred[512]{0:T(512)(128)(4,1)S(1)} %fusion.63), kind=kOutput, calls=%fused_computation.7 | convolution fusion | flops 1613004800 | bytes 17961472 | tf_op jit(solution)/shard_map/dot_general | solution.py:38
  147.9 4.3 select_select_fusion.3
  152.2 10.4 %scatter.14 = f32[4096,512]{1,0:T(8,128)} dynamic-update-slice(f32[4096,512]{1,0:T(8,128)} %copy-done.2, f32[4096,64]{1,0:T(8,128)S(1)} %select_select_fusion.3, s32[]{:T(128)} %constant.151.clone.1, s32[]{:T(128)} %constant.151.clone.1) | dynamic-update-slice | bytes 2097156 | tf_op jit(solution)/shard_map/scatter | solution.py:75
  164.3 21.7 %all-reduce.13.cloned.1.call-done = f32[64,512]{1,0:T(8,128)} async-done(((f32[64,512]{1,0:T(8,128)}), f32[64,512]{1,0:T(8,128)}) %all-reduce.13.cloned.1.call-update) | async-done | bytes 131088 | tf_op jit(solution)/shard_map/psum | solution.py:13
  188.4 4.7 convolution_select_fusion.2
  194.1 96.2 %all-reduce.15.cloned.1.call-done = f32[64,4096]{0,1:T(8,128)} async-done(((f32[64,4096]{0,1:T(8,128)}), f32[64,4096]{0,1:T(8,128)}) %all-reduce.15.cloned.1.call-update) | async-done | bytes 1048592 | tf_op jit(solution)/shard_map/psum | solution.py:13
  290.3 9.6 %convolution_subtract_fusion.2 = f32[4096,512]{1,0:T(8,128)S(1)} fusion(f32[4096,512]{1,0:T(8,128)} %scatter.14, f32[64,4096]{0,1:T(8,128)} %all-reduce.15.cloned.1.call-done, pred[4096]{0:T(1024)(128)(4,1)S(1)} %fusion.58, f32[64,512]{1,0:T(8,128)S(1)} %copy-done.10, pred[512]{0:T(512)(128)(4,1)S(1)} %fusion.62), kind=kOutput, calls=%fused_computation.6 | convolution fusion | flops 1613004800 | bytes 17961472 | tf_op jit(solution)/shard_map/dot_general | solution.py:38
  303.1 4.3 select_select_fusion.2
  307.5 12.0 %scatter.15 = f32[4096,512]{1,0:T(8,128)} dynamic-update-slice(f32[4096,512]{1,0:T(8,128)} %copy-done, f32[4096,64]{1,0:T(8,128)S(1)} %select_select_fusion.2, s32[]{:T(128)} %constant.151.clone.1, s32[]{:T(128)} %constant.147.clone.1) | dynamic-update-slice | bytes 2097156 | tf_op jit(solution)/shard_map/scatter | solution.py:75
  321.1 21.7 %all-reduce.17.cloned.1.call-done = f32[64,512]{1,0:T(8,128)} async-done(((f32[64,512]{1,0:T(8,128)}), f32[64,512]{1,0:T(8,128)}) %all-reduce.17.cloned.1.call-update) | async-done | bytes 131088 | tf_op jit(solution)/shard_map/psum | solution.py:13
  345.2 4.7 convolution_select_fusion.1
  350.7 96.3 %all-reduce.19.cloned.1.call-done = f32[64,4096]{0,1:T(8,128)} async-done(((f32[64,4096]{0,1:T(8,128)}), f32[64,4096]{0,1:T(8,128)}) %all-reduce.19.cloned.1.call-update) | async-done | bytes 1048592 | tf_op jit(solution)/shard_map/psum | solution.py:13
  447.0 9.6 %convolution_subtract_fusion.1 = f32[4096,512]{1,0:T(8,128)S(1)} fusion(f32[4096,512]{1,0:T(8,128)} %scatter.15, f32[64,4096]{0,1:T(8,128)} %all-reduce.19.cloned.1.call-done, pred[4096]{0:T(1024)(128)(4,1)S(1)} %fusion.57, f32[64,512]{1,0:T(8,128)S(1)} %copy-done.11, pred[512]{0:T(512)(128)(4,1)S(1)} %fusion.61), kind=kOutput, calls=%fused_computation.5 | convolution fusion | flops 1613004800 | bytes 17961472 | tf_op jit(solution)/shard_map/dot_general | solution.py:38
  459.9 4.2 select_select_fusion.1
  464.1 10.6 %scatter.16 = f32[4096,512]{1,0:T(8,128)} dynamic-update-slice(f32[4096,512]{1,0:T(8,128)} %copy-done.1, f32[4096,64]{1,0:T(8,128)S(1)} %select_select_fusion.1, s32[]{:T(128)} %constant.151.clone.1, s32[]{:T(128)} %constant.158.clone.1) | dynamic-update-slice | bytes 2097156 | tf_op jit(solution)/shard_map/scatter | solution.py:75
  476.6 21.5 %all-reduce.21.cloned.1.call-done = f32[64,512]{1,0:T(8,128)} async-done(((f32[64,512]{1,0:T(8,128)}), f32[64,512]{1,0:T(8,128)}) %all-reduce.21.cloned.1.call-update) | async-done | bytes 131088 | tf_op jit(solution)/shard_map/psum | solution.py:13
  500.5 4.8 convolution_select_fusion
  506.0 96.4 %all-reduce.23.cloned.1.call-done = f32[64,4096]{0,1:T(8,128)} async-done(((f32[64,4096]{0,1:T(8,128)}), f32[64,4096]{0,1:T(8,128)}) %all-reduce.23.cloned.1.call-update) | async-done | bytes 1048592 | tf_op jit(solution)/shard_map/psum | solution.py:13
  602.4 9.6 %convolution_subtract_fusion = f32[4096,512]{1,0:T(8,128)S(1)} fusion(f32[4096,512]{1,0:T(8,128)} %scatter.16, f32[64,4096]{0,1:T(8,128)} %all-reduce.23.cloned.1.call-done, pred[4096]{0:T(1024)(128)(4,1)S(1)} %fusion.56, f32[64,512]{1,0:T(8,128)S(1)} %copy-done.9, pred[512]{0:T(512)(128)(4,1)S(1)} %fusion.60), kind=kOutput, calls=%fused_computation.4 | convolution fusion | flops 1613004800 | bytes 17961472 | tf_op jit(solution)/shard_map/dot_general | solution.py:38
  615.5 4.4 select_select_fusion
  619.8 11.9 %scatter.19 = f32[4096,512]{1,0:T(8,128)} dynamic-update-slice(f32[4096,512]{1,0:T(8,128)} %copy-done.3, f32[4096,64]{1,0:T(8,128)S(1)} %select_select_fusion, s32[]{:T(128)} %constant.151.clone.1, s32[]{:T(128)} %constant.159.clone.1) | dynamic-update-slice | bytes 2097156 | tf_op jit(solution)/shard_map/scatter | solution.py:75
  (85 shorter events, 32.6 us)
Async XLA Ops:
  6.5 24.1 %all-reduce.9.cloned.1.call-start = ((), (), s32[]{:S(2)}) async-start(), calls=%async_computation | async-start | bytes 262144 | tf_op jit(solution)/shard_map/psum | solution.py:13
  8.1 126.7 %all-reduce.11.cloned.1.call-start = ((), (), s32[]{:S(2)}) async-start(), calls=%async_computation.1 | async-start | bytes 4194304 | tf_op jit(solution)/shard_map/psum | solution.py:13
  37.8 97.1 %copy-start.8 = (f32[64,512]{1,0:T(8,128)S(1)}, f32[64,512]{1,0:T(8,128)}, u32[]{:S(2)}) copy-start(f32[64,512]{1,0:T(8,128)} %all-reduce.9.cloned.1.call-done) | copy-start | bytes 393220
  37.8 148.2 %all-reduce.13.cloned.1.call-start = ((), (), s32[]{:S(2)}) async-start(), calls=%async_computation.2 | async-start | bytes 262144 | tf_op jit(solution)/shard_map/psum | solution.py:13
  134.8 13.0 %copy-start.4 = (f32[64,4096]{0,1:T(8,128)S(1)}, f32[64,4096]{0,1:T(8,128)}, u32[]{:S(2)}) copy-start(f32[64,4096]{0,1:T(8,128)} %all-reduce.11.cloned.1.call-done) | copy-start | bytes 3145732
  144.5 3.4 copy-start.2
  164.2 126.1 %all-reduce.15.cloned.1.call-start = ((), (), s32[]{:S(2)}) async-start(), calls=%async_computation.3 | async-start | bytes 4194304 | tf_op jit(solution)/shard_map/psum | solution.py:13
  193.2 97.1 %copy-start.10 = (f32[64,512]{1,0:T(8,128)S(1)}, f32[64,512]{1,0:T(8,128)}, u32[]{:S(2)}) copy-start(f32[64,512]{1,0:T(8,128)} %all-reduce.13.cloned.1.call-done) | copy-start | bytes 393220
  193.2 149.6 %all-reduce.17.cloned.1.call-start = ((), (), s32[]{:S(2)}) async-start(), calls=%async_computation.4 | async-start | bytes 262144 | tf_op jit(solution)/shard_map/psum | solution.py:13
  290.3 12.9 %copy-start.6 = (f32[64,4096]{0,1:T(8,128)S(1)}, f32[64,4096]{0,1:T(8,128)}, u32[]{:S(2)}) copy-start(f32[64,4096]{0,1:T(8,128)} %all-reduce.15.cloned.1.call-done) | copy-start | bytes 3145732
  299.9 3.2 copy-start
  321.1 125.9 %all-reduce.19.cloned.1.call-start = ((), (), s32[]{:S(2)}) async-start(), calls=%async_computation.5 | async-start | bytes 4194304 | tf_op jit(solution)/shard_map/psum | solution.py:13
  349.9 97.1 %copy-start.11 = (f32[64,512]{1,0:T(8,128)S(1)}, f32[64,512]{1,0:T(8,128)}, u32[]{:S(2)}) copy-start(f32[64,512]{1,0:T(8,128)} %all-reduce.17.cloned.1.call-done) | copy-start | bytes 393220
  349.9 148.1 %all-reduce.21.cloned.1.call-start = ((), (), s32[]{:S(2)}) async-start(), calls=%async_computation.6 | async-start | bytes 262144 | tf_op jit(solution)/shard_map/psum | solution.py:13
  447.0 12.9 %copy-start.7 = (f32[64,4096]{0,1:T(8,128)S(1)}, f32[64,4096]{0,1:T(8,128)}, u32[]{:S(2)}) copy-start(f32[64,4096]{0,1:T(8,128)} %all-reduce.19.cloned.1.call-done) | copy-start | bytes 3145732
  456.6 3.2 copy-start.1
  476.3 126.1 %all-reduce.23.cloned.1.call-start = ((), (), s32[]{:S(2)}) async-start(), calls=%async_computation.7 | async-start | bytes 4194304 | tf_op jit(solution)/shard_map/psum | solution.py:13
  505.3 97.1 %copy-start.9 = (f32[64,512]{1,0:T(8,128)S(1)}, f32[64,512]{1,0:T(8,128)}, u32[]{:S(2)}) copy-start(f32[64,512]{1,0:T(8,128)} %all-reduce.21.cloned.1.call-done) | copy-start | bytes 393220
  602.4 13.0 %copy-start.5 = (f32[64,4096]{0,1:T(8,128)S(1)}, f32[64,4096]{0,1:T(8,128)}, u32[]{:S(2)}) copy-start(f32[64,4096]{0,1:T(8,128)} %all-reduce.23.cloned.1.call-done) | copy-start | bytes 3145732
  612.1 3.4 copy-start.3
Sparse Core Ops, SparseCore 0:
  9.6 21.0 all-reduce.8
  37.9 96.8 all-reduce.10
  164.3 21.6 all-reduce.12
  193.3 96.9 all-reduce.14
  321.2 21.6 all-reduce.16
  350.1 96.8 all-reduce.18
  476.4 21.6 all-reduce.20
  505.4 96.9 all-reduce.22
where the time goes:
time: 645 us; the launch traced here: 639 us
  waiting for transfers between devices  473 us (73%)
  local copies, waits for them, and re-layouts  61.4 us (10%)
  matrix products  60.6 us (9%)
  other arithmetic  29.4 us (5%)
  between operations  13.8 us (2%)
    psum x8, waiting for transfers between devices, spread(): return lax.psum(jnp.where(mine, x, jnp.zeros_like(x)), axis)  473 us
    scatter x4, local copies, waits for them, and re-layouts, per_device(): share = share.at[:, offset:offset + B].set(new_column)  44.9 us
    dot_general x4, matrix products, trailing_drop(): lax.dot_general(lower_used, upper_used, (((0,), (0,)), ((), ())), precisi...  38.5 us
    another operation x8, other arithmetic  19.9 us
    dot_general x4, matrix products, lower_rows(): lax.dot_general(inverse, column_slab, (((0,), (1,)), ((), ())), precision...  18.9 us
    unnamed x24, local copies, waits for them, and re-layouts  13.2 us
  transfers between devices with their start and end apart: 8, of which 8 were waited for; matrix products, arithmetic and copies ran while one was open for 0% of the time, Pallas kernels for 0%

commit v1 on v0

v1 whole, which is shorter than its diff:
```python
import functools

import jax
import jax.numpy as jnp
from jax import lax
from jax.experimental import pallas as pl
from jax.experimental.pallas import tpu as pltpu
from jax.sharding import PartitionSpec as P

B = 64
P_SIZE = 256
PIECE = 64
UNIT = 256
LEAD = 4
MESH = pl.DeviceIdType.MESH


def exact_dot(left, right):
    return jnp.dot(left, right, precision=lax.Precision.HIGHEST, preferred_element_type=jnp.float32)


def split(x):
    high = x.astype(jnp.bfloat16)
    low = (x - high.astype(jnp.float32)).astype(jnp.bfloat16)
    return high, low


def fused_dot(left, right):
    return jnp.dot(left, right, preferred_element_type=jnp.float32)


def kernel(
    layers, front, panel, out,
    held, share, rows_in, pivot, inner, x_buf, t_buf, g_high, g_low,
    recv_sem, rows_sem, load_sem, out_sem, send_sem,
):
    height, width = share.shape
    half = UNIT // 2
    pivot_pieces = P_SIZE // 2 // PIECE
    unit_pieces = half // PIECE
    units = height // UNIT
    total = pivot_pieces + units * unit_pieces
    order = list(range(pivot_pieces, pivot_pieces + LEAD)) + list(range(pivot_pieces))
    order += list(range(pivot_pieces + LEAD, total))

    r, col, z = lax.axis_index("row"), lax.axis_index("col"), lax.axis_index("layer")
    y, core = col // 2, col % 2
    flat = col * layers + z
    root_chip = jnp.logical_and(y == 0, z == 0)
    root = jnp.logical_and(root_chip, core == 0)
    has_sib = jnp.logical_not(jnp.logical_and(root_chip, core == 1))

    def device(row, yy, cc, zz):
        return (row, yy * 2 + cc, zz)

    along = jnp.logical_and(y == core, z < layers - 1)
    back = jnp.logical_and(jnp.logical_and(core == 0, y == 1), z == 1)
    has_one = jnp.logical_or(along, back)
    one = device(r, y, core, jnp.where(back, 0, jnp.minimum(z + 1, layers - 1)))
    has_two = jnp.logical_and(y == core, z >= 1)
    two = device(r, 1 - y, core, z)
    sib = device(r, y, 1 - core, z)
    tree_b = device(r, 1, 1, 0)
    other = device(1 - r, y, core, z)

    at_start = z == 0
    parent_y = jnp.where(at_start, jnp.where(core == 0, 1, 0), jnp.where(y == core, y, 1 - y))
    parent_z = jnp.where(at_start, jnp.where(core == 0, 1, 0), jnp.where(y == core, z - 1, z))
    parent_core = jnp.where(at_start, 0, core)
    barrier = pltpu.get_barrier_semaphore()

    @pl.when(jnp.logical_not(root_chip))
    def _():
        pl.semaphore_signal(
            barrier, inc=1, device_id=device(r, parent_y, parent_core, parent_z), device_id_type=MESH
        )

    @pl.when(jnp.logical_not(root))
    def _():
        pl.semaphore_signal(barrier, inc=1, device_id=sib, device_id_type=MESH)

    @pl.when(r == 1)
    def _():
        pl.semaphore_signal(barrier, inc=1, device_id=other, device_id_type=MESH)

    def row_of(t, i):
        return ((i - pivot_pieces) // unit_pieces) * UNIT + t * half + ((i - pivot_pieces) % unit_pieces) * PIECE

    @pl.when(root)
    def _():
        for i in order:
            for t in range(2):
                if i < pivot_pieces:
                    @pl.when(r == 0)
                    def _():
                        pltpu.make_async_copy(
                            panel.at[pl.ds(t * half + i * PIECE, PIECE), pl.ds(0, P_SIZE)],
                            held.at[t, pl.ds(i * PIECE, PIECE)],
                            recv_sem.at[t, i],
                        ).start()
                else:
                    pltpu.make_async_copy(
                        panel.at[pl.ds(row_of(t, i), PIECE), pl.ds(0, P_SIZE)],
                        held.at[t, pl.ds(i * PIECE, PIECE)],
                        recv_sem.at[t, i],
                    ).start()

    load = pltpu.make_async_copy(front, share, load_sem)
    load.start()

    @pl.when(r == 0)
    def _():
        pltpu.make_async_copy(front.at[pl.ds(0, P_SIZE)], rows_in, rows_sem).start()

    peers = (
        has_sib.astype(jnp.int32) + has_one.astype(jnp.int32) + has_two.astype(jnp.int32)
        + root.astype(jnp.int32) + (r == 0).astype(jnp.int32)
    )
    pl.when(peers > 0)(lambda: pl.semaphore_wait(barrier, peers))

    def piece(t, i, kind, target):
        return pltpu.make_async_remote_copy(
            src_ref=held.at[t, pl.ds(i * PIECE, PIECE)],
            dst_ref=held.at[t, pl.ds(i * PIECE, PIECE)],
            send_sem=send_sem.at[kind],
            recv_sem=recv_sem.at[t, i],
            device_id=target,
            device_id_type=MESH,
        )

    def arrived(t, i):
        pltpu.make_async_copy(
            held.at[t, pl.ds(i * PIECE, PIECE)], held.at[t, pl.ds(i * PIECE, PIECE)], recv_sem.at[t, i]
        ).wait()

    def forward(i):
        arrived(core, i)

        @pl.when(has_one)
        def _():
            piece(core, i, 0, one).start()

        @pl.when(has_two)
        def _():
            piece(core, i, 1, two).start()

        @pl.when(has_sib)
        def _():
            piece(core, i, 2, sib).start()

        @pl.when(root)
        def _():
            arrived(1, i)
            piece(1, i, 3, tree_b).start()
            piece(1, i, 4, sib).start()

    def pivot_piece_across(t, i):
        return pltpu.make_async_remote_copy(
            src_ref=panel.at[pl.ds(t * half + i * PIECE, PIECE), pl.ds(0, P_SIZE)],
            dst_ref=held.at[t, pl.ds(i * PIECE, PIECE)],
            send_sem=send_sem.at[5 + t],
            recv_sem=recv_sem.at[t, i],
            device_id=other,
            device_id_type=MESH,
        )

    @pl.when(jnp.logical_and(root, r == 0))
    def _():
        for i in range(pivot_pieces):
            for t in range(2):
                pivot_piece_across(t, i).start()

    def rows_across():
        return pltpu.make_async_remote_copy(
            src_ref=front.at[pl.ds(0, P_SIZE)],
            dst_ref=rows_in,
            send_sem=send_sem.at[7],
            recv_sem=rows_sem,
            device_id=other,
            device_id_type=MESH,
        )

    def other_arrived(i):
        @pl.when(jnp.logical_not(root))
        def _():
            arrived(1 - core, i)

    queue = list(order)

    def forward_some(count):
        for _ in range(min(count, len(queue))):
            forward(queue.pop(0))

    forward_some(LEAD + pivot_pieces)

    @pl.when(r == 0)
    def _():
        rows_across().start()

    for i in range(pivot_pieces):
        other_arrived(i)
    pivot[pl.ds(0, half), :] = held[0, pl.ds(0, half), :]
    pivot[pl.ds(half, half), :] = held[1, pl.ds(0, half), :]
    inner[...] = jnp.zeros_like(inner)

    eye = lax.broadcasted_iota(jnp.int32, (B, B), 0) == lax.broadcasted_iota(jnp.int32, (B, B), 1)
    blocks = P_SIZE // B
    for k in range(blocks):
        lo, hi = k * B, (k + 1) * B
        d = pivot[lo:hi, lo:hi]
        diagonal = jnp.where(eye, d, 0.0)
        down = 1.0 / jnp.sum(diagonal, axis=1, keepdims=True)
        across = 1.0 / jnp.sum(diagonal, axis=0, keepdims=True)
        x = jnp.where(eye, 2.0 * down, 0.0) - down * (d * across)
        x_buf[...] = x
        t_buf[...] = exact_dot(d, x)
        forward_some(1)
        x = x_buf[...]
        x = 2.0 * x - exact_dot(x, t_buf[...])
        x_buf[...] = x
        inner[lo:hi, lo:hi] = x
        forward_some(1)
        x = x_buf[...]
        if k < blocks - 1:
            pivot[hi:, lo:hi] = exact_dot(pivot[hi:, lo:hi], x)
            forward_some(1)
        if k > 0:
            inner[0:lo, lo:hi] = -exact_dot(exact_dot(inner[0:lo, 0:lo], pivot[0:lo, lo:hi]), x)
            forward_some(1)
        if k < blocks - 1:
            lower = pivot[hi:, lo:hi]
            pivot[hi:, hi:] = pivot[hi:, hi:] - exact_dot(lower, pivot[lo:hi, hi:])
            forward_some(1)
            if k == 0:
                pltpu.make_async_copy(rows_in, rows_in, rows_sem).wait()
            rows_in[hi:, :] = rows_in[hi:, :] - exact_dot(lower, rows_in[lo:hi, :])
            forward_some(1)

    owned = min(width, P_SIZE)
    g = exact_dot(inner[...], rows_in[...])
    high, low = split(g)
    g_high[...] = high
    g_low[...] = low
    for f in range(P_SIZE // owned):
        @pl.when(flat == f)
        def _():
            high, low = split(-inner[:, f * owned : (f + 1) * owned])
            g_high[:, 0:owned] = high
            g_low[:, 0:owned] = low
            rows_in[:, 0:owned] = pivot[:, f * owned : (f + 1) * owned]

    load.wait()
    kept = flat * width + lax.broadcasted_iota(jnp.int32, (half, width), 1) >= P_SIZE

    def update(u):
        for j in range(unit_pieces):
            other_arrived(pivot_pieces + u * unit_pieces + j)
        start = pivot_pieces * PIECE + u * half
        if not isinstance(u, int):
            start = pl.multiple_of(start, PIECE)
        for t in range(2):
            high, low = split(held[t, pl.ds(start, half), :])
            drop = fused_dot(high, g_high[...]) + fused_dot(high, g_low[...]) + fused_dot(low, g_high[...])
            place = pl.ds(u * UNIT + t * half, half)
            share[place, :] = jnp.where(kept, share[place, :], 0.0) - drop

        pltpu.make_async_copy(
            share.at[pl.ds(u * UNIT, UNIT)], out.at[pl.ds(u * UNIT, UNIT)], out_sem
        ).start()

    @pl.when(r == 0)
    def _():
        for j in range(unit_pieces):
            other_arrived(pivot_pieces + j)
        share[0:UNIT, :] = rows_in[...]
        pltpu.make_async_copy(share.at[pl.ds(0, UNIT)], out.at[pl.ds(0, UNIT)], out_sem).start()

    @pl.when(r != 0)
    def _():
        update(0)

    done = 1
    rest = len(queue)
    first = queue[0] if rest else 0

    def step(s, carry):
        forward(first + s)
        update(done + s)
        return carry

    beside = min(rest, units - 1)
    lax.fori_loop(0, beside, step, 0)
    if rest > beside:
        lax.fori_loop(first + beside, first + rest, lambda i, c: (forward(i), c)[1], 0)
    lax.fori_loop(done + beside, units, lambda u, c: (update(u), c)[1], 0)

    def sent(t, kind):
        pltpu.make_async_copy(held.at[t], held.at[t], send_sem.at[kind]).wait()

    pl.when(has_one)(lambda: sent(0, 0))
    pl.when(has_two)(lambda: sent(0, 1))
    pl.when(has_sib)(lambda: sent(0, 2))

    @pl.when(root)
    def _():
        sent(1, 3)
        sent(1, 4)

    @pl.when(jnp.logical_and(root, r == 0))
    def _():
        for t in range(2):
            pltpu.make_async_copy(
                held.at[t, pl.ds(0, half)], held.at[t, pl.ds(0, half)], send_sem.at[5 + t]
            ).wait()

    @pl.when(r == 0)
    def _():
        rows_across().wait_send()

    pltpu.make_async_copy(share, out, out_sem).wait()


def per_device(layers, front):
    height, width = front.shape
    panel = front
    if width < P_SIZE:
        parts = [front] + [
            lax.ppermute(front, ("col", "layer"), [(f, 0)]) for f in range(1, P_SIZE // width)
        ]
        panel = jnp.concatenate(parts, axis=1)
    pieces = (P_SIZE + height) // 2 // PIECE
    hbm = pl.BlockSpec(memory_space=pl.ANY)
    return pl.pallas_call(
        functools.partial(kernel, layers),
        out_shape=jax.ShapeDtypeStruct((height, width), jnp.float32),
        in_specs=[hbm, hbm],
        out_specs=hbm,
        scratch_shapes=[
            pltpu.VMEM((2, (P_SIZE + height) // 2, P_SIZE), jnp.float32),
            pltpu.VMEM((height, width), jnp.float32),
            pltpu.VMEM((P_SIZE, width), jnp.float32),
            pltpu.VMEM((P_SIZE, P_SIZE), jnp.float32),
            pltpu.VMEM((P_SIZE, P_SIZE), jnp.float32),
            pltpu.VMEM((B, B), jnp.float32),
            pltpu.VMEM((B, B), jnp.float32),
            pltpu.VMEM((P_SIZE, width), jnp.bfloat16),
            pltpu.VMEM((P_SIZE, width), jnp.bfloat16),
            pltpu.SemaphoreType.DMA((2, pieces)),
            pltpu.SemaphoreType.DMA,
            pltpu.SemaphoreType.DMA,
            pltpu.SemaphoreType.DMA,
            pltpu.SemaphoreType.DMA((8,)),
        ],
        compiler_params=pltpu.CompilerParams(
            collective_id=0, has_side_effects=True, vmem_limit_bytes=40 * 1024 * 1024
        ),
        cost_estimate=pl.CostEstimate(
            flops=6 * height * width * P_SIZE, bytes_accessed=8 * height * width, transcendentals=0
        ),
    )(front, panel)


def solution(mesh):
    placed = (P("row", ("col", "layer")),)
    return jax.shard_map(
        functools.partial(per_device, mesh.shape["layer"]),
        mesh=mesh,
        in_specs=placed,
        out_specs=P("row", ("col", "layer")),
        check_vma=False,
    )
```

time: 645 us -> 55.1 us (0.09)
  waiting for transfers between devices: 473 us -> 0 us
  matrix products: 60.6 us -> 0 us
  local copies, waits for them, and re-layouts: 61.4 us -> 3.4 us
  Pallas kernels: 0 us -> 51.5 us
  other arithmetic: 29.4 us -> 0 us
  between operations: 13.8 us -> 0.01 us
    psum x8 -> x0, waiting for transfers between devices: 473 us -> none  [spread(): return lax.psum(jnp.where(mine, x, jnp.zeros_like(x)), axis)]
    dot_general x24 -> x0, matrix products: 60.6 us -> none  [the longest x4 38.5 us: trailing_drop(): lax.dot_general(lower_used, upper_used, (((0,), (0,)), ((), ())), precisi...]
    pallas_call x0 -> x1, Pallas kernels: none -> 51.5 us  [per_device(): pl.pallas_call(functools.partial(kernel, layers), out_shape=jax.ShapeDtyp...]
    scatter x4 -> x0, local copies, waits for them, and re-layouts: 44.9 us -> none  [per_device(): share = share.at[:, offset:offset + B].set(new_column)]
    another operation x8 -> x0, other arithmetic: 19.9 us -> none
    unnamed x24 -> x1, local copies, waits for them, and re-layouts: 13.2 us -> 3.4 us
    select_n x8 -> x0, other arithmetic: 9.47 us -> none  [the longest x4 6.27 us: spread(): return lax.psum(jnp.where(mine, x, jnp.zeros_like(x)), axis)]
  transfers between devices with their start and end apart: 8 -> 0, of which waited for: 8 -> 0; matrix products, arithmetic and copies ran while one was open for 0% -> 0% of each run, Pallas kernels for 0% -> 0%
where the time goes in v1:
time: 55.1 us; the launch traced here: 54.9 us
  Pallas kernels  51.5 us (93%)
  local copies, waits for them, and re-layouts  3.4 us (6%)
    pallas_call x1, Pallas kernels, per_device(): pl.pallas_call(functools.partial(kernel, layers), out_shape=jax.ShapeDtyp...  51.5 us
    unnamed x1, local copies, waits for them, and re-layouts  3.4 us

profile of v1, /device:TPU:27, one launch (start us, length us, event | category | flops | bytes accessed | tf_op | source)
XLA Modules:
  0.0 54.9 jit_solution(8928434300023741917)
XLA Ops:
  0.0 51.5 %shard_map.17 = f32[4096,512]{1,0:T(8,128)S(1)} custom-call(f32[4096,512]{1,0:T(8,128)} %panel.1, f32[4096,512]{1,0:T(8,128)} %panel.1), custom_call_target="tpu_custom_call" | custom-call | flops 3221225472 | bytes 16777216 | tf_op jit(solution)/shard_map/pallas_call | solution.py:333
  51.5 3.4 %copy.3 = f32[4096,512]{1,0:T(8,128)} copy(f32[4096,512]{1,0:T(8,128)S(1)} %shard_map.17) | data formatting | bytes 16777216

commit v2 on v1

--- a/solution.py
+++ b/solution.py
@@ -11,7 +11,9 @@
 P_SIZE = 256
 PIECE = 64
 UNIT = 256
-LEAD = 4
+LEAD = 6
+LAG = 8
+EVERY = 2
 MESH = pl.DeviceIdType.MESH
 
 
@@ -30,13 +32,13 @@
 
 
 def kernel(
-    layers, front, panel, out,
-    held, share, rows_in, pivot, inner, x_buf, t_buf, g_high, g_low,
-    recv_sem, rows_sem, load_sem, out_sem, send_sem,
+    layers, front, panel, share,
+    held, rows_in, pivot, inner, x_buf, t_buf, g_high, g_low,
+    recv_sem, rows_sem, load_sem, send_sem,
 ):
     height, width = share.shape
     half = UNIT // 2
-    pivot_pieces = P_SIZE // 2 // PIECE
+    pivot_pieces = P_SIZE // PIECE
     unit_pieces = half // PIECE
     units = height // UNIT
     total = pivot_pieces + units * unit_pieces
@@ -88,17 +90,17 @@
 
     @pl.when(root)
     def _():
-        for i in order:
+        for i in sorted(order):
             for t in range(2):
-                if i < pivot_pieces:
+                if i < pivot_pieces and t == 0:
                     @pl.when(r == 0)
                     def _():
                         pltpu.make_async_copy(
-                            panel.at[pl.ds(t * half + i * PIECE, PIECE), pl.ds(0, P_SIZE)],
-                            held.at[t, pl.ds(i * PIECE, PIECE)],
-                            recv_sem.at[t, i],
+                            panel.at[pl.ds(i * PIECE, PIECE), pl.ds(0, P_SIZE)],
+                            held.at[0, pl.ds(i * PIECE, PIECE)],
+                            recv_sem.at[0, i],
                         ).start()
-                else:
+                elif i >= pivot_pieces:
                     pltpu.make_async_copy(
                         panel.at[pl.ds(row_of(t, i), PIECE), pl.ds(0, P_SIZE)],
                         held.at[t, pl.ds(i * PIECE, PIECE)],
@@ -118,9 +120,9 @@
     )
     pl.when(peers > 0)(lambda: pl.semaphore_wait(barrier, peers))
 
-    def piece(t, i, kind, target):
+    def piece(t, i, kind, target, source=None):
         return pltpu.make_async_remote_copy(
-            src_ref=held.at[t, pl.ds(i * PIECE, PIECE)],
+            src_ref=held.at[t if source is None else source, pl.ds(i * PIECE, PIECE)],
             dst_ref=held.at[t, pl.ds(i * PIECE, PIECE)],
             send_sem=send_sem.at[kind],
             recv_sem=recv_sem.at[t, i],
@@ -134,7 +136,11 @@
         ).wait()
 
     def forward(i):
-        arrived(core, i)
+        is_pivot = isinstance(i, int) and i < pivot_pieces
+        if is_pivot:
+            pl.when(jnp.logical_not(first_root))(lambda: arrived(core, i))
+        else:
+            arrived(core, i)
 
         @pl.when(has_one)
         def _():
@@ -144,37 +150,31 @@
         def _():
             piece(core, i, 1, two).start()
 
-        @pl.when(has_sib)
-        def _():
-            piece(core, i, 2, sib).start()
+        if not is_pivot:
+            @pl.when(has_sib)
+            def _():
+                piece(core, i, 2, sib).start()
 
         @pl.when(root)
         def _():
-            arrived(1, i)
-            piece(1, i, 3, tree_b).start()
-            piece(1, i, 4, sib).start()
-
-    def pivot_piece_across(t, i):
-        return pltpu.make_async_remote_copy(
-            src_ref=panel.at[pl.ds(t * half + i * PIECE, PIECE), pl.ds(0, P_SIZE)],
-            dst_ref=held.at[t, pl.ds(i * PIECE, PIECE)],
-            send_sem=send_sem.at[5 + t],
-            recv_sem=recv_sem.at[t, i],
-            device_id=other,
-            device_id_type=MESH,
-        )
-
-    @pl.when(jnp.logical_and(root, r == 0))
+            if not is_pivot:
+                arrived(1, i)
+            piece(1, i, 3, tree_b, 0 if is_pivot else None).start()
+            piece(1, i, 4, sib, 0 if is_pivot else None).start()
+
+    first_root = jnp.logical_and(root, r == 0)
+
+    @pl.when(first_root)
     def _():
         for i in range(pivot_pieces):
-            for t in range(2):
-                pivot_piece_across(t, i).start()
+            arrived(0, i)
+            piece(0, i, 5, other).start()
 
     def rows_across():
         return pltpu.make_async_remote_copy(
             src_ref=front.at[pl.ds(0, P_SIZE)],
             dst_ref=rows_in,
-            send_sem=send_sem.at[7],
+            send_sem=send_sem.at[6],
             recv_sem=rows_sem,
             device_id=other,
             device_id_type=MESH,
@@ -186,21 +186,28 @@
             arrived(1 - core, i)
 
     queue = list(order)
+    stages = [0]
+
+    def stage_done():
+        stages[0] += 1
+        if stages[0] % EVERY == 0:
+            forward_some(1)
 
     def forward_some(count):
         for _ in range(min(count, len(queue))):
             forward(queue.pop(0))
 
+    @pl.when(jnp.logical_and(r == 0, has_sib))
+    def _():
+        rows_across().start()
+
     forward_some(LEAD + pivot_pieces)
 
-    @pl.when(r == 0)
+    @pl.when(jnp.logical_and(r == 0, jnp.logical_not(has_sib)))
     def _():
         rows_across().start()
 
-    for i in range(pivot_pieces):
-        other_arrived(i)
-    pivot[pl.ds(0, half), :] = held[0, pl.ds(0, half), :]
-    pivot[pl.ds(half, half), :] = held[1, pl.ds(0, half), :]
+    pivot[...] = held[core, pl.ds(0, P_SIZE), :]
     inner[...] = jnp.zeros_like(inner)
 
     eye = lax.broadcasted_iota(jnp.int32, (B, B), 0) == lax.broadcasted_iota(jnp.int32, (B, B), 1)
@@ -214,27 +221,29 @@
         x = jnp.where(eye, 2.0 * down, 0.0) - down * (d * across)
         x_buf[...] = x
         t_buf[...] = exact_dot(d, x)
-        forward_some(1)
+        stage_done()
         x = x_buf[...]
         x = 2.0 * x - exact_dot(x, t_buf[...])
         x_buf[...] = x
         inner[lo:hi, lo:hi] = x
-        forward_some(1)
+        stage_done()
         x = x_buf[...]
         if k < blocks - 1:
             pivot[hi:, lo:hi] = exact_dot(pivot[hi:, lo:hi], x)
-            forward_some(1)
+            stage_done()
         if k > 0:
             inner[0:lo, lo:hi] = -exact_dot(exact_dot(inner[0:lo, 0:lo], pivot[0:lo, lo:hi]), x)
-            forward_some(1)
+            stage_done()
         if k < blocks - 1:
             lower = pivot[hi:, lo:hi]
             pivot[hi:, hi:] = pivot[hi:, hi:] - exact_dot(lower, pivot[lo:hi, hi:])
-            forward_some(1)
-            if k == 0:
-                pltpu.make_async_copy(rows_in, rows_in, rows_sem).wait()
-            rows_in[hi:, :] = rows_in[hi:, :] - exact_dot(lower, rows_in[lo:hi, :])
-            forward_some(1)
+            stage_done()
+
+    pltpu.make_async_copy(rows_in, rows_in, rows_sem).wait()
+    for k in range(blocks - 1):
+        lo, hi = k * B, (k + 1) * B
+        rows_in[hi:, :] = rows_in[hi:, :] - exact_dot(pivot[hi:, lo:hi], rows_in[lo:hi, :])
+        stage_done()
 
     owned = min(width, P_SIZE)
     g = exact_dot(inner[...], rows_in[...])
@@ -264,34 +273,47 @@
             place = pl.ds(u * UNIT + t * half, half)
             share[place, :] = jnp.where(kept, share[place, :], 0.0) - drop
 
-        pltpu.make_async_copy(
-            share.at[pl.ds(u * UNIT, UNIT)], out.at[pl.ds(u * UNIT, UNIT)], out_sem
-        ).start()
-
     @pl.when(r == 0)
     def _():
         for j in range(unit_pieces):
             other_arrived(pivot_pieces + j)
         share[0:UNIT, :] = rows_in[...]
-        pltpu.make_async_copy(share.at[pl.ds(0, UNIT)], out.at[pl.ds(0, UNIT)], out_sem).start()
 
     @pl.when(r != 0)
     def _():
         update(0)
 
+    step_pieces = unit_pieces // 2
+    forward_some(len(queue) % step_pieces)
+    first = total - len(queue)
+    halves = len(queue) // step_pieces
+    here = 2 * units - halves
     done = 1
-    rest = len(queue)
-    first = queue[0] if rest else 0
-
-    def step(s, carry):
-        forward(first + s)
+    behind = 0
+    lag = LAG // step_pieces
+    while behind < halves and done + 2 * (behind + 1) <= (here + behind + 1 - lag) // 2:
+        behind += 1
+
+    def catch_up(s, carry):
+        for j in range(step_pieces):
+            forward(first + s * step_pieces + j)
+        update(done + 2 * s)
+        update(done + 2 * s + 1)
+        return carry
+
+    lax.fori_loop(0, behind, catch_up, 0)
+    first, halves, done = first + behind * step_pieces, halves - behind, done + 2 * behind
+
+    def level(s, carry):
+        for j in range(unit_pieces):
+            forward(first + s * unit_pieces + j)
         update(done + s)
         return carry
 
-    beside = min(rest, units - 1)
-    lax.fori_loop(0, beside, step, 0)
-    if rest > beside:
-        lax.fori_loop(first + beside, first + rest, lambda i, c: (forward(i), c)[1], 0)
+    beside = min(halves // 2, units - done)
+    lax.fori_loop(0, beside, level, 0)
+    for i in range(first + beside * unit_pieces, total):
+        forward(i)
     lax.fori_loop(done + beside, units, lambda u, c: (update(u), c)[1], 0)
 
     def sent(t, kind):
@@ -299,7 +321,11 @@
 
     pl.when(has_one)(lambda: sent(0, 0))
     pl.when(has_two)(lambda: sent(0, 1))
-    pl.when(has_sib)(lambda: sent(0, 2))
+
+    @pl.when(has_sib)
+    def _():
+        whole = held.at[0, pl.ds(P_SIZE, height // 2)]
+        pltpu.make_async_copy(whole, whole, send_sem.at[2]).wait()
 
     @pl.when(root)
     def _():
@@ -308,16 +334,13 @@
 
     @pl.when(jnp.logical_and(root, r == 0))
     def _():
-        for t in range(2):
-            pltpu.make_async_copy(
-                held.at[t, pl.ds(0, half)], held.at[t, pl.ds(0, half)], send_sem.at[5 + t]
-            ).wait()
+        pltpu.make_async_copy(
+            held.at[0, pl.ds(0, P_SIZE)], held.at[0, pl.ds(0, P_SIZE)], send_sem.at[5]
+        ).wait()
 
     @pl.when(r == 0)
     def _():
         rows_across().wait_send()
-
-    pltpu.make_async_copy(share, out, out_sem).wait()
 
 
 def per_device(layers, front):
@@ -328,16 +351,15 @@
             lax.ppermute(front, ("col", "layer"), [(f, 0)]) for f in range(1, P_SIZE // width)
         ]
         panel = jnp.concatenate(parts, axis=1)
-    pieces = (P_SIZE + height) // 2 // PIECE
+    pieces = (P_SIZE + height // 2) // PIECE
     hbm = pl.BlockSpec(memory_space=pl.ANY)
     return pl.pallas_call(
         functools.partial(kernel, layers),
         out_shape=jax.ShapeDtypeStruct((height, width), jnp.float32),
         in_specs=[hbm, hbm],
-        out_specs=hbm,
+        out_specs=pl.BlockSpec(memory_space=pltpu.VMEM),
         scratch_shapes=[
-            pltpu.VMEM((2, (P_SIZE + height) // 2, P_SIZE), jnp.float32),
-            pltpu.VMEM((height, width), jnp.float32),
+            pltpu.VMEM((2, P_SIZE + height // 2, P_SIZE), jnp.float32),
             pltpu.VMEM((P_SIZE, width), jnp.float32),
             pltpu.VMEM((P_SIZE, P_SIZE), jnp.float32),
             pltpu.VMEM((P_SIZE, P_SIZE), jnp.float32),
@@ -348,8 +370,7 @@
             pltpu.SemaphoreType.DMA((2, pieces)),
             pltpu.SemaphoreType.DMA,
             pltpu.SemaphoreType.DMA,
-            pltpu.SemaphoreType.DMA,
-            pltpu.SemaphoreType.DMA((8,)),
+            pltpu.SemaphoreType.DMA((7,)),
         ],
         compiler_params=pltpu.CompilerParams(
             collective_id=0, has_side_effects=True, vmem_limit_bytes=40 * 1024 * 1024

time: 55.1 us -> 51 us (0.926)
  Pallas kernels: 51.5 us -> 47.4 us
    pallas_call x1, Pallas kernels: 51.5 us -> 47.4 us  [per_device(): pl.pallas_call(functools.partial(kernel, layers), out_shape=jax.ShapeDtyp...]
where the time goes in v2:
time: 51 us; the launch traced here: 50.8 us
  Pallas kernels  47.4 us (93%)
  local copies, waits for them, and re-layouts  3.4 us (7%)
    pallas_call x1, Pallas kernels, per_device(): pl.pallas_call(functools.partial(kernel, layers), out_shape=jax.ShapeDtyp...  47.4 us
    unnamed x1, local copies, waits for them, and re-layouts  3.4 us

profile of v2, /device:TPU:27, one launch (start us, length us, event | category | flops | bytes accessed | tf_op | source)
XLA Modules:
  0.0 50.8 jit_solution(6041269097759133358)
XLA Ops:
  0.0 47.4 %shard_map.17 = f32[4096,512]{1,0:T(8,128)S(1)} custom-call(f32[4096,512]{1,0:T(8,128)} %panel.1, f32[4096,512]{1,0:T(8,128)} %panel.1), custom_call_target="tpu_custom_call" | custom-call | flops 3221225472 | bytes 16777216 | tf_op jit(solution)/shard_map/pallas_call | solution.py:356
  47.4 3.4 %copy.3 = f32[4096,512]{1,0:T(8,128)} copy(f32[4096,512]{1,0:T(8,128)S(1)} %shard_map.17) | data formatting | bytes 16777216
